TPU v7x, 32 devices: a whole 2x2x4 slice. The times are simulated.
32 devices in a mesh: seq: 8 (over z, x), head: 4 (over y, core).
Axes of the slice: x: 2, y: 2, z: 4, core: 2. Of those that a mesh axis runs over, the one named last changes fastest.
Arguments:
- query: bfloat16 [2048, 1024], P('seq', 'head'), may hold values from -20 to 20
- key_states: bfloat16 [2048, 1024], P('seq', 'head'), may hold values from -20 to 20
- values: bfloat16 [2048, 1024], P('seq', 'head'), may hold values from -6 to 6
- grad_out: bfloat16 [2048, 1024], P('seq', 'head'), may hold values from -6 to 6
- rand_blocks: int32 [32, 2], replicated, may hold values from 0 to 31, as said below
- global_blocks: int32 [2], replicated, may hold values from 0 to 31, as said below
Outputs:
- out: bfloat16 [2048, 1024], P('seq', 'head')
- dq: bfloat16 [2048, 1024], P('seq', 'head')
- dk: bfloat16 [2048, 1024], P('seq', 'head')
- dv: bfloat16 [2048, 1024], P('seq', 'head')
Inputs may be any that keep to these rules, and one draw needn't show every extreme that they name: `rand_blocks`: take the query blocks of one index of seq (aligned runs of 4 rows). Among their 8 entries at most 2 lie in the blocks of any one index o (blocks o*4 to o*4 + 3), and for every run some index receives exactly 2 of them. `global_blocks`: 2 different block numbers; the last of them is the sequence's last block.
All inputs are finite; a program needn't handle non-finite values.
Results may differ from a plain program's by a relative error of at most 0.04.
Values may be sent and summed in bfloat16 or wider, within the bound.
A program may use at most 128 MiB of HBM per device.

v0:
```python
import math
import jax
import jax.numpy as jnp
from jax import lax
from jax.sharding import PartitionSpec as P

HEAD_SIZE = 128
BLOCK_TOKENS = 64


def extended_2(block, sides, width):
    for axis, dim in sides:
        count = lax.axis_size(axis)
        forward = [(i, i + 1) for i in range(count - 1)]
        forward.append((count - 1, 0))
        backward = [(target, source) for source, target in forward]
        low = lax.ppermute(
            lax.slice_in_dim(block, block.shape[dim] - width, None, axis=dim), axis, forward
        )
        high = lax.ppermute(lax.slice_in_dim(block, 0, width, axis=dim), axis, backward)
        block = jnp.concatenate([low, block, high], axis=dim)
    return block


def shards(query, key_states, values, grad_out, rand_blocks, global_blocks):
    tokens, feature_width = query.shape
    head_count = feature_width // HEAD_SIZE
    nshard = lax.axis_size("seq")
    myself = lax.axis_index("seq")
    block_count = tokens // BLOCK_TOKENS
    nrand = rand_blocks.shape[1]
    nglob = global_blocks.shape[0]
    nfixed = 3 + nglob
    needed = block_count * nrand
    slots = max(2, (needed + nshard - 1) // nshard)
    double_width = 2 * feature_width
    score_scale = 1.0 / math.sqrt(HEAD_SIZE)
    paired = jnp.concatenate([key_states, values], axis=1)
    paired_blocks = paired.reshape(block_count, BLOCK_TOKENS, double_width)
    extended = extended_2(paired, (("seq", 0),), BLOCK_TOKENS)
    owners_glob = global_blocks // block_count
    local_glob = global_blocks % block_count
    pieces = []
    for glob_index in range(nglob):
        piece = lax.dynamic_slice_in_dim(
            paired, local_glob[glob_index] * BLOCK_TOKENS, BLOCK_TOKENS, 0
        )
        pieces.append(jnp.where(owners_glob[glob_index] == myself, piece.astype(jnp.float32), 0.0))
    global_rows = lax.psum(jnp.concatenate(pieces, axis=0), "seq").astype(jnp.bfloat16)
    table = rand_blocks.reshape(nshard, needed)
    owner_table = table // block_count
    local_table = table % block_count
    position = jnp.arange(needed)
    earlier_same = (owner_table[:, :, None] == owner_table[:, None, :]) & (
        position[None, None, :] < position[None, :, None]
    )
    rank_table = jnp.sum(earlier_same.astype(jnp.int32), axis=2)
    slot_range = jnp.arange(slots)
    matched = (owner_table[:, :, None] == myself) & (
        rank_table[:, :, None] == slot_range[None, None, :]
    )
    valid = jnp.any(matched, axis=1)
    send_local = jnp.sum(jnp.where(matched, local_table[:, :, None], 0), axis=1)
    outgoing = jnp.where(
        valid[:, :, None, None], paired_blocks[send_local], jnp.zeros((), jnp.bfloat16)
    )
    incoming = lax.all_to_all(outgoing, "seq", split_axis=0, concat_axis=0, tiled=True)
    my_owner = lax.dynamic_index_in_dim(owner_table, myself, 0, keepdims=False)
    my_rank = lax.dynamic_index_in_dim(rank_table, myself, 0, keepdims=False)
    flat_slot = my_owner * slots + my_rank
    fetched = incoming.reshape(nshard * slots, BLOCK_TOKENS, double_width)[flat_slot].reshape(
        block_count, nrand, BLOCK_TOKENS, double_width
    )
    ext_blocks = extended.reshape(block_count + 2, BLOCK_TOKENS, double_width)
    window_blocks = jnp.stack([ext_blocks[:-2], ext_blocks[1:-1], ext_blocks[2:]], axis=1)
    glob_wide = jnp.broadcast_to(
        global_rows.reshape(1, nglob, BLOCK_TOKENS, double_width),
        (block_count, nglob, BLOCK_TOKENS, double_width),
    )
    gathered = jnp.concatenate([window_blocks, glob_wide, fetched], axis=1)
    key_count = gathered.shape[1]
    key_matrix = gathered[..., :feature_width].reshape(
        block_count, key_count * BLOCK_TOKENS, head_count, HEAD_SIZE
    )
    value_matrix = gathered[..., feature_width:].reshape(
        block_count, key_count * BLOCK_TOKENS, head_count, HEAD_SIZE
    )
    query_matrix = query.reshape(block_count, BLOCK_TOKENS, head_count, HEAD_SIZE)
    logit_scores = (
        jnp.einsum("bqhd,bkhd->bhqk", query_matrix, key_matrix, preferred_element_type=jnp.float32)
        * score_scale
    )
    top = jnp.max(logit_scores, axis=-1, keepdims=True)
    lse = top + jnp.log(jnp.sum(jnp.exp(logit_scores - top), axis=-1, keepdims=True))
    probs = jnp.exp(logit_scores - lse)
    softmax_weights = probs.astype(jnp.bfloat16)
    attended_output = jnp.einsum(
        "bhqk,bkhd->bqhd", softmax_weights, value_matrix, preferred_element_type=jnp.float32
    ).astype(jnp.bfloat16)
    out = attended_output.reshape(tokens, feature_width)
    gradient_rows = grad_out.reshape(block_count, BLOCK_TOKENS, head_count, HEAD_SIZE)
    delta = jnp.sum(gradient_rows.astype(jnp.float32) * attended_output.astype(jnp.float32), axis=3)
    delta = jnp.transpose(delta, (0, 2, 1))[..., None]
    probability_gradient = jnp.einsum(
        "bqhd,bkhd->bhqk", gradient_rows, value_matrix, preferred_element_type=jnp.float32
    )
    dscore = (probs * (probability_gradient - delta) * score_scale).astype(jnp.bfloat16)
    query_gradient = jnp.einsum(
        "bhqk,bkhd->bqhd", dscore, key_matrix, preferred_element_type=jnp.float32
    ).astype(jnp.bfloat16)
    query_gradient = query_gradient.reshape(tokens, feature_width)
    key_term = jnp.einsum(
        "bhqk,bqhd->bkhd", dscore, query_matrix, preferred_element_type=jnp.float32
    )
    value_term = jnp.einsum(
        "bhqk,bqhd->bkhd", softmax_weights, gradient_rows, preferred_element_type=jnp.float32
    )
    terms = jnp.concatenate(
        [
            key_term.reshape(block_count, key_count, BLOCK_TOKENS, feature_width),
            value_term.reshape(block_count, key_count, BLOCK_TOKENS, feature_width),
        ],
        axis=3,
    )
    zero_one = jnp.zeros((1, BLOCK_TOKENS, double_width), jnp.float32)
    zero_two = jnp.zeros((2, BLOCK_TOKENS, double_width), jnp.float32)
    ext_grad = (
        jnp.concatenate([terms[:, 0], zero_two], axis=0)
        + jnp.concatenate([zero_one, terms[:, 1], zero_one], axis=0)
        + jnp.concatenate([zero_two, terms[:, 2]], axis=0)
    )
    rims = jnp.concatenate([ext_grad[0], ext_grad[-1]], axis=0)
    returned = extended_2(rims, (("seq", 0),), BLOCK_TOKENS)
    own = ext_grad[1:-1]
    own = own.at[0].add(returned[:BLOCK_TOKENS]).at[-1].add(returned[3 * BLOCK_TOKENS :])
    glob_terms = jnp.sum(terms[:, 3:nfixed], axis=0)
    glob_total = lax.psum(glob_terms, "seq")
    block_ids = jnp.arange(block_count)
    for glob_index in range(nglob):
        owned_here = (block_ids == local_glob[glob_index]) & (owners_glob[glob_index] == myself)
        own = own + jnp.where(owned_here[:, None, None], glob_total[glob_index][None], 0.0)
    tile_terms = terms[:, nfixed:].reshape(needed, BLOCK_TOKENS, double_width).astype(jnp.bfloat16)
    empty = jnp.zeros((nshard * slots,) + tile_terms.shape[1:], tile_terms.dtype)
    arrived = lax.all_to_all(
        empty.at[flat_slot].set(tile_terms).reshape((nshard, slots) + tile_terms.shape[1:]),
        "seq",
        split_axis=0,
        concat_axis=0,
        tiled=True,
    )
    selector = (send_local.reshape(-1)[None, :] == block_ids[:, None]) & valid.reshape(-1)[None, :]
    own = own + jnp.einsum(
        "bs,sqc->bqc",
        selector.astype(jnp.bfloat16),
        arrived.reshape(nshard * slots, BLOCK_TOKENS, double_width),
        preferred_element_type=jnp.float32,
    )
    own = own.reshape(tokens, double_width)
    dkey = own[:, :feature_width].astype(jnp.bfloat16)
    dvalue = own[:, feature_width:].astype(jnp.bfloat16)
    return (out, query_gradient, dkey, dvalue)


def solution(mesh):
    in_specs = (P("seq", "head"), P("seq", "head"), P("seq", "head"), P("seq", "head"), P(), P())
    out_specs = (P("seq", "head"), P("seq", "head"), P("seq", "head"), P("seq", "head"))
    return jax.shard_map(shards, mesh=mesh, in_specs=in_specs, out_specs=out_specs, check_vma=False)
```

profile of v0, /device:TPU:0, one launch (start us, length us, event | category | flops | bytes accessed | tf_op | source)
XLA Modules:
  0.0 201.1 jit_solution(15153234952446303233)
XLA Ops:
  7.2 0.9 constant_dynamic-update-slice_fusion.1
  8.1 0.8 copy.73
  9.8 0.9 constant_dynamic-update-slice_fusion
  10.7 0.6 gather_fusion
  11.4 1.1 broadcast_select_fusion
  12.5 7.4 %all-to-all-start = ((bf16[8,2,64,512]{3,2,1,0:T(8,128)(2,1)}), bf16[8,2,64,512]{3,2,1,0:T(8,128)(2,1)S(1)}, u32[]{:S(2)}, u32[]{:S(2)}) async-start(bf16[8,2,64,512]{3,2,1,0:T(8,128)(2,1)} %broadcast_select_fusion), calls=%async_computation | async-start | bytes 2097152 | tf_op jit(solution)/shard_map/all_to_all | solution.py:67
  19.9 4.8 %collective-permute-start.1 = (bf16[64,512]{1,0:T(8,128)(2,1)S(1)}, bf16[64,512]{1,0:T(8,128)(2,1)S(1)}, u32[]{:S(2)}, u32[]{:S(2)}) collective-permute-start(bf16[64,512]{1,0:T(8,128)(2,1)S(1)} %get-tuple-element.45), channel_id=1, source_target_pairs={{4,0},{8,4},{12,8},{16,12},{20,16},{24,20},{28,24},{0,28},{5,1},{9... | collective-permute-start | bytes 196616 | tf_op jit(solution)/shard_map/ppermute | solution.py:20
  24.7 0.6 fusion.46
  28.3 45.0 %all-reduce.6 = bf16[128,512]{1,0:T(8,128)(2,1)S(1)} all-reduce(f32[128,512]{1,0:T(8,128)S(1)} %pad_maximum_fusion.3), channel_id=1, replica_groups=mesh['seq'=8,'head'=4] {'seq'}, use_global_device_ids=true, to_apply=%region_0.1 | all-reduce | flops 65536 | bytes 393216 | tf_op jit(solution)/shard_map/psum | solution.py:49
  73.5 0.8 constant_dynamic-update-slice_fusion.5
  74.2 0.7 constant_dynamic-update-slice_fusion.4
  75.0 0.7 constant_dynamic-update-slice_fusion.3
  75.7 0.8 broadcast_dynamic-update-slice_fusion
  76.5 0.6 gather_fusion.1
  77.1 0.9 constant_dynamic-update-slice_fusion.2
  78.0 1.6 fusion.43
  79.6 1.1 reshape.302
  80.9 0.6 fusion.48
  81.9 0.7 convolution_bitcast_fusion
  82.7 1.1 multiply_reduce_fusion
  83.8 0.5 fusion.4
  84.3 2.7 %copy.91 = f32[4,448,2,128]{3,2,1,0:T(2,128)} copy(f32[4,448,2,128]{3,1,2,0:T(8,128)S(1)} %convolution_bitcast_fusion) | data formatting | bytes 3670016 | tf_op jit(solution)/shard_map/bhqk,bqhd->bkhd/transpose | solution.py:115
  87.0 2.7 %reshape.309 = f32[4,7,64,256]{3,2,1,0:T(8,128)S(1)} reshape(f32[4,448,2,128]{3,2,1,0:T(2,128)} %copy.91) | data formatting | bytes 3670016 | tf_op jit(solution)/shard_map/reshape | solution.py:121
  90.2 2.7 %copy.89 = f32[4,448,2,128]{3,2,1,0:T(2,128)} copy(f32[4,448,2,128]{3,1,2,0:T(8,128)S(1)} %convolution_bitcast_fusion.1) | data formatting | bytes 3670016 | tf_op jit(solution)/shard_map/bhqk,bqhd->bkhd/transpose | solution.py:112
  92.9 3.6 %reshape.308 = f32[4,7,64,256]{3,2,1,0:T(8,128)} reshape(f32[4,448,2,128]{3,2,1,0:T(2,128)} %copy.89) | data formatting | bytes 3670016 | tf_op jit(solution)/shard_map/reshape | solution.py:120
  96.5 2.0 pad_maximum_fusion
  98.5 1.8 copy-done
  100.6 0.8 scatter_fusion
  101.4 2.1 %copy.99 = bf16[8,2,64,512]{3,1,2,0:T(2,128)(2,1)} copy(bf16[8,2,64,512]{3,2,1,0:T(8,128)(2,1)S(1)} %bitcast.105) | data formatting | bytes 2097152 | tf_op jit(solution)/shard_map/reshape | solution.py:145
  103.4 4.5 %all-to-all-start.1 = ((bf16[8,2,64,512]{3,1,2,0:T(2,128)(2,1)}), bf16[8,2,64,512]{3,1,2,0:T(2,128)(2,1)S(1)}, u32[]{:S(2)}, u32[]{:S(2)}) async-start(bf16[8,2,64,512]{3,1,2,0:T(2,128)(2,1)} %copy.99), calls=%async_computation.1 | async-start | bytes 2097152 | tf_op jit(solution)/shard_map/all_to_all | solution.py:144
  108.2 0.7 compare_and_fusion
  108.8 0.7 compare_and_fusion.1
  109.5 1.6 fusion.42
  111.2 0.6 copy-done.2
  111.9 0.7 fusion.17
  112.5 1.8 collective-permute-start.2
  114.3 2.0 %copy_reduce_fusion = f32[2,64,512]{2,1,0:T(8,128)} fusion(f32[4,7,64,512]{3,2,1,0:T(8,128)} %copy-done), kind=kLoop, calls=%fused_computation.18 | loop fusion | flops 196608 | bytes 1310720 | tf_op jit(solution)/shard_map/reduce_sum | solution.py:136
  116.4 1.4 fusion.6
  117.8 1.2 fusion.12
  119.2 0.7 copy.146
  120.0 0.7 copy.145
  120.7 7.4 %collective-permute-done.2 = f32[64,512]{1,0:T(8,128)} collective-permute-done((f32[64,512]{1,0:T(8,128)}, f32[64,512]{1,0:T(8,128)}, u32[]{:S(2)}, u32[]{:S(2)}) %collective-permute-start.2) | collective-permute-done | bytes 131104 | tf_op jit(solution)/shard_map/ppermute | solution.py:17
  128.1 1.0 fusion.21
  129.5 59.6 %all-reduce.5.cloned.1.call-done = f32[2,64,512]{2,1,0:T(8,128)} async-done(((f32[2,64,512]{2,1,0:T(8,128)}), f32[2,64,512]{2,1,0:T(8,128)}) %all-reduce.5.cloned.1.call-update) | async-done | bytes 262160 | tf_op jit(solution)/shard_map/psum | solution.py:137
  189.0 1.0 slice_bitcast_fusion.1
  190.2 1.3 scatter-add.9
  191.5 1.1 copy.100
  193.6 0.7 fusion.44
  (69 shorter events, 5.0 us)
Async XLA Ops:
  11.4 13.3 %copy-start.8 = (s32[2]{0:T(128)S(1)}, s32[2]{0:T(128)}, u32[]{:S(2)}) copy-start(s32[2]{0:T(128)} %param.15) | copy-start | bytes 28
  11.4 15.4 %copy-start.6 = (bf16[256,256]{1,0:T(8,128)(2,1)S(1)}, bf16[256,256]{1,0:T(8,128)(2,1)}, u32[]{:S(2)}) copy-start(bf16[256,256]{1,0:T(8,128)(2,1)} %param.13) | copy-start | bytes 393220
  12.5 15.7 %copy-start.7 = (bf16[256,256]{1,0:T(8,128)(2,1)S(1)}, bf16[256,256]{1,0:T(8,128)(2,1)}, u32[]{:S(2)}) copy-start(bf16[256,256]{1,0:T(8,128)(2,1)} %param.10) | copy-start | bytes 393220
  12.5 64.0 %all-to-all-start = ((bf16[8,2,64,512]{3,2,1,0:T(8,128)(2,1)}), bf16[8,2,64,512]{3,2,1,0:T(8,128)(2,1)S(1)}, u32[]{:S(2)}, u32[]{:S(2)}) async-start(bf16[8,2,64,512]{3,2,1,0:T(8,128)(2,1)} %broadcast_select_fusion), calls=%async_computation | async-start | bytes 2097152 | tf_op jit(solution)/shard_map/all_to_all | solution.py:67
  19.9 53.5 %collective-permute-start.1 = (bf16[64,512]{1,0:T(8,128)(2,1)S(1)}, bf16[64,512]{1,0:T(8,128)(2,1)S(1)}, u32[]{:S(2)}, u32[]{:S(2)}) collective-permute-start(bf16[64,512]{1,0:T(8,128)(2,1)S(1)} %get-tuple-element.45), channel_id=1, source_target_pairs={{4,0},{8,4},{12,8},{16,12},{20,16},{24,20},{28,24},{0,28},{5,1},{9... | collective-permute-start | bytes 196616 | tf_op jit(solution)/shard_map/ppermute | solution.py:20
  24.7 48.7 %collective-permute-start = (bf16[64,512]{1,0:T(8,128)(2,1)S(1)}, bf16[64,512]{1,0:T(8,128)(2,1)S(1)}, u32[]{:S(2)}, u32[]{:S(2)}) collective-permute-start(bf16[64,512]{1,0:T(8,128)(2,1)S(1)} %get-tuple-element.46), channel_id=1, source_target_pairs={{0,4},{4,8},{8,12},{12,16},{16,20},{20,24},{24,28},{28,0},{1,5},{5... | collective-permute-start | bytes 196616 | tf_op jit(solution)/shard_map/ppermute | solution.py:17
  81.5 1.2 copy-start.1
  84.3 5.4 %copy-start.4 = (bf16[4,2,64,448]{3,2,1,0:T(8,128)(2,1)}, bf16[4,2,64,448]{3,2,1,0:T(8,128)(2,1)S(1)}, u32[]{:S(2)}) copy-start(bf16[4,2,64,448]{3,2,1,0:T(8,128)(2,1)S(1)} %fusion.4) | copy-start | bytes 1376260
  98.5 1.8 copy-start
  103.4 88.1 %all-to-all-start.1 = ((bf16[8,2,64,512]{3,1,2,0:T(2,128)(2,1)}), bf16[8,2,64,512]{3,1,2,0:T(2,128)(2,1)S(1)}, u32[]{:S(2)}, u32[]{:S(2)}) async-start(bf16[8,2,64,512]{3,1,2,0:T(2,128)(2,1)} %copy.99), calls=%async_computation.1 | async-start | bytes 2097152 | tf_op jit(solution)/shard_map/all_to_all | solution.py:144
  107.9 81.1 %all-reduce.5.cloned.1.call-start = ((), (), s32[]{:S(2)}) async-start(), calls=%async_computation.2 | async-start | bytes 524288 | tf_op jit(solution)/shard_map/psum | solution.py:137
  111.2 0.7 copy-start.2
  112.5 15.6 %collective-permute-start.2 = (f32[64,512]{1,0:T(8,128)}, f32[64,512]{1,0:T(8,128)}, u32[]{:S(2)}, u32[]{:S(2)}) collective-permute-start(f32[64,512]{1,0:T(8,128)} %fusion.17), channel_id=1, source_target_pairs={{0,4},{4,8},{8,12},{12,16},{16,20},{20,24},{24,28},{28,0},{1,5},{5... | collective-permute-start | bytes 393224 | tf_op jit(solution)/shard_map/ppermute | solution.py:17
  116.4 2.7 %copy-start.5 = (bf16[4,64,2,128]{3,1,2,0:T(8,128)(2,1)S(1)}, bf16[4,64,2,128]{3,1,2,0:T(8,128)(2,1)}, u32[]{:S(2)}) copy-start(bf16[4,64,2,128]{3,1,2,0:T(8,128)(2,1)} %get-tuple-element.56) | copy-start | bytes 393220
  117.8 10.3 %copy-start.3 = (f32[1,64,512]{2,1,0:T(8,128)S(1)}, f32[1,64,512]{2,1,0:T(8,128)}, u32[]{:S(2)}) copy-start(f32[1,64,512]{2,1,0:T(8,128)} %copy-done.2) | copy-start | bytes 393220
  129.4 60.6 %collective-permute-start.3 = (f32[64,512]{1,0:T(8,128)S(1)}, f32[64,512]{1,0:T(8,128)S(1)}, u32[]{:S(2)}, u32[]{:S(2)}) collective-permute-start(f32[64,512]{1,0:T(8,128)S(1)} %get-tuple-element.35), channel_id=1, source_target_pairs={{4,0},{8,4},{12,8},{16,12},{20,16},{24,20},{28,24},{0,28},{5,1},{9... | collective-permute-start | bytes 393224 | tf_op jit(solution)/shard_map/ppermute | solution.py:20
Sparse Core Ops, SparseCore 0:
  116.5 72.4 all-reduce.4
where the time goes:
time: 202 us; the launch traced here: 201 us
  waiting for transfers between devices  67 us (33%)
  blocking collectives  45 us (22%)
  local copies, waits for them, and re-layouts  37.5 us (19%)
  starting transfers between devices  18.8 us (9%)
  between operations  17.1 us (8%)
  other arithmetic  10.5 us (5%)
  matrix products  5.15 us (3%)
    psum x1, waiting for transfers between devices, shards(): glob_total = lax.psum(glob_terms, 'seq')  59.6 us
    psum x1, blocking collectives, shards(): lax.psum(jnp.concatenate(pieces, axis=0), 'seq').astype(jnp.bfloat16)  45 us
    unnamed x30, local copies, waits for them, and re-layouts  8.83 us
    all_to_all x1, starting transfers between devices, shards(): lax.all_to_all(outgoing, 'seq', split_axis=0, concat_axis=0, tiled=True)  7.38 us
    ppermute x2, waiting for transfers between devices, extended_2(): lax.ppermute(lax.slice_in_dim(block, block.shape[dim] - width, None, axis...  7.38 us
    ppermute x2, starting transfers between devices, extended_2(): lax.ppermute(lax.slice_in_dim(block, 0, width, axis=dim), axis, backward)  4.83 us
    all_to_all x1, starting transfers between devices, shards(): lax.all_to_all(empty.at[flat_slot].set(tile_terms).reshape((nshard, slots...  4.53 us
  transfers between devices with their start and end apart: 7, of which 2 were waited for; matrix products, arithmetic and copies ran while one was open for 9% of the time, Pallas kernels for 0%

commit v1 on v0

--- a/solution.py
+++ b/solution.py
@@ -134,7 +134,7 @@
     own = ext_grad[1:-1]
     own = own.at[0].add(returned[:BLOCK_TOKENS]).at[-1].add(returned[3 * BLOCK_TOKENS :])
     glob_terms = jnp.sum(terms[:, 3:nfixed], axis=0)
-    glob_total = lax.psum(glob_terms, "seq")
+    glob_total = jnp.sum(lax.all_gather(glob_terms, "seq"), 0)
     block_ids = jnp.arange(block_count)
     for glob_index in range(nglob):
         owned_here = (block_ids == local_glob[glob_index]) & (owners_glob[glob_index] == myself)

time: 202 us -> 174 us (0.86)
  waiting for transfers between devices: 67 us -> 41.2 us
    psum x1 -> x0, waiting for transfers between devices: 59.6 us -> none  [shards(): glob_total = lax.psum(glob_terms, 'seq')]
    ppermute x2, waiting for transfers between devices: 7.38 us -> 22 us  [extended_2(): lax.ppermute(lax.slice_in_dim(block, block.shape[dim] - width, None, axis...]
    all_gather x0 -> x1, waiting for transfers between devices: none -> 14.1 us  [shards(): glob_total = jnp.sum(lax.all_gather(glob_terms, 'seq'), 0)]
    ppermute x2, waiting for transfers between devices: 0.01 us -> 5.1 us  [extended_2(): lax.ppermute(lax.slice_in_dim(block, 0, width, axis=dim), axis, backward)]
    unnamed x30 -> x28, local copies, waits for them, and re-layouts: 8.83 us -> 8.94 us
  transfers between devices with their start and end apart: 7 -> 7, of which waited for: 2 -> 3; matrix products, arithmetic and copies ran while one was open for 9% -> 10% of each run, Pallas kernels for 0% -> 0%
where the time goes in v1:
time: 174 us; the launch traced here: 173 us
  blocking collectives  45.3 us (26%)
  waiting for transfers between devices  41.2 us (24%)
  local copies, waits for them, and re-layouts  38 us (22%)
  starting transfers between devices  18.8 us (11%)
  between operations  17.1 us (10%)
  other arithmetic  8.53 us (5%)
  matrix products  4.07 us (2%)
    psum x1, blocking collectives, shards(): lax.psum(jnp.concatenate(pieces, axis=0), 'seq').astype(jnp.bfloat16)  45.3 us
    ppermute x2, waiting for transfers between devices, extended_2(): lax.ppermute(lax.slice_in_dim(block, block.shape[dim] - width, None, axis...  22 us
    all_gather x1, waiting for transfers between devices, shards(): glob_total = jnp.sum(lax.all_gather(glob_terms, 'seq'), 0)  14.1 us
    unnamed x28, local copies, waits for them, and re-layouts  8.94 us
    all_to_all x1, starting transfers between devices, shards(): lax.all_to_all(outgoing, 'seq', split_axis=0, concat_axis=0, tiled=True)  7.38 us
    ppermute x2, waiting for transfers between devices, extended_2(): lax.ppermute(lax.slice_in_dim(block, 0, width, axis=dim), axis, backward)  5.1 us
    ppermute x2, starting transfers between devices, extended_2(): lax.ppermute(lax.slice_in_dim(block, 0, width, axis=dim), axis, backward)  4.78 us
    all_to_all x1, starting transfers between devices, shards(): lax.all_to_all(empty.at[flat_slot].set(tile_terms).reshape((nshard, slots...  4.53 us
  transfers between devices with their start and end apart: 7, of which 3 were waited for; matrix products, arithmetic and copies ran while one was open for 10% of the time, Pallas kernels for 0%

profile of v1, /device:TPU:0, one launch (start us, length us, event | category | flops | bytes accessed | tf_op | source)
XLA Modules:
  0.0 173.0 jit_solution(3258275549879798393)
XLA Ops:
  7.2 0.9 constant_dynamic-update-slice_fusion.1
  8.1 0.8 copy.73
  9.8 0.9 constant_dynamic-update-slice_fusion
  10.7 0.6 gather_fusion
  11.4 1.1 broadcast_select_fusion
  12.5 7.4 %all-to-all-start = ((bf16[8,2,64,512]{3,2,1,0:T(8,128)(2,1)}), bf16[8,2,64,512]{3,2,1,0:T(8,128)(2,1)S(1)}, u32[]{:S(2)}, u32[]{:S(2)}) async-start(bf16[8,2,64,512]{3,2,1,0:T(8,128)(2,1)} %broadcast_select_fusion), calls=%async_computation | async-start | bytes 2097152 | tf_op jit(solution)/shard_map/all_to_all | solution.py:67
  20.0 4.7 %collective-permute-start.1 = (bf16[64,512]{1,0:T(8,128)(2,1)S(1)}, bf16[64,512]{1,0:T(8,128)(2,1)S(1)}, u32[]{:S(2)}, u32[]{:S(2)}) collective-permute-start(bf16[64,512]{1,0:T(8,128)(2,1)S(1)} %get-tuple-element.45), channel_id=1, source_target_pairs={{4,0},{8,4},{12,8},{16,12},{20,16},{24,20},{28,24},{0,28},{5,1},{9... | collective-permute-start | bytes 196616 | tf_op jit(solution)/shard_map/ppermute | solution.py:20
  24.7 0.6 fusion.46
  28.1 45.3 %all-reduce.3 = bf16[128,512]{1,0:T(8,128)(2,1)S(1)} all-reduce(f32[128,512]{1,0:T(8,128)S(1)} %pad_maximum_fusion.3), channel_id=1, replica_groups=mesh['seq'=8,'head'=4] {'seq'}, use_global_device_ids=true, to_apply=%region_0.1 | all-reduce | flops 65536 | bytes 393216 | tf_op jit(solution)/shard_map/psum | solution.py:49
  73.5 0.8 constant_dynamic-update-slice_fusion.5
  74.2 0.7 constant_dynamic-update-slice_fusion.4
  74.9 0.7 constant_dynamic-update-slice_fusion.3
  75.7 0.8 broadcast_dynamic-update-slice_fusion
  76.5 0.6 gather_fusion.1
  77.1 0.9 constant_dynamic-update-slice_fusion.2
  78.0 1.6 fusion.43
  79.6 1.1 reshape.302
  80.9 0.6 fusion.48
  81.9 0.7 convolution_bitcast_fusion
  82.7 1.1 multiply_reduce_fusion
  83.8 0.5 fusion.4
  84.4 2.7 %copy.91 = f32[4,448,2,128]{3,2,1,0:T(2,128)} copy(f32[4,448,2,128]{3,1,2,0:T(8,128)S(1)} %convolution_bitcast_fusion) | data formatting | bytes 3670016 | tf_op jit(solution)/shard_map/bhqk,bqhd->bkhd/transpose | solution.py:115
  87.0 2.7 %reshape.309 = f32[4,7,64,256]{3,2,1,0:T(8,128)S(1)} reshape(f32[4,448,2,128]{3,2,1,0:T(2,128)} %copy.91) | data formatting | bytes 3670016 | tf_op jit(solution)/shard_map/reshape | solution.py:121
  89.8 0.5 convolution_bitcast_fusion.1
  90.2 2.7 %copy.89 = f32[4,448,2,128]{3,2,1,0:T(2,128)} copy(f32[4,448,2,128]{3,1,2,0:T(8,128)S(1)} %convolution_bitcast_fusion.1) | data formatting | bytes 3670016 | tf_op jit(solution)/shard_map/bhqk,bqhd->bkhd/transpose | solution.py:112
  92.9 3.6 %reshape.308 = f32[4,7,64,256]{3,2,1,0:T(8,128)} reshape(f32[4,448,2,128]{3,2,1,0:T(2,128)} %copy.89) | data formatting | bytes 3670016 | tf_op jit(solution)/shard_map/reshape | solution.py:120
  96.5 2.0 %pad_maximum_fusion = f32[4,7,64,512]{3,2,1,0:T(8,128)S(1)} fusion(f32[4,7,64,256]{3,2,1,0:T(8,128)S(1)} %reshape.309, f32[4,7,64,256]{3,2,1,0:T(8,128)} %reshape.308), kind=kLoop, calls=%fused_computation.3 | loop fusion | flops 917504 | bytes 7340032 | tf_op jit(solution)/shard_map/concatenate | solution.py:118
  98.5 1.8 %copy-done = f32[4,7,64,512]{3,2,1,0:T(8,128)} copy-done((f32[4,7,64,512]{3,2,1,0:T(8,128)}, f32[4,7,64,512]{3,2,1,0:T(8,128)S(1)}, u32[]{:S(2)}) %copy-start) | copy-done | bytes 3670040
  100.3 0.8 copy_reduce_fusion
  101.1 1.3 slice.164
  102.6 0.8 scatter_fusion
  103.4 2.1 %copy.99 = bf16[8,2,64,512]{3,1,2,0:T(2,128)(2,1)} copy(bf16[8,2,64,512]{3,2,1,0:T(8,128)(2,1)S(1)} %bitcast.106) | data formatting | bytes 2097152 | tf_op jit(solution)/shard_map/reshape | solution.py:145
  105.5 4.5 %all-to-all-start.1 = ((bf16[8,2,64,512]{3,1,2,0:T(2,128)(2,1)}), bf16[8,2,64,512]{3,1,2,0:T(2,128)(2,1)S(1)}, u32[]{:S(2)}, u32[]{:S(2)}) async-start(bf16[8,2,64,512]{3,1,2,0:T(2,128)(2,1)} %copy.99), calls=%async_computation.1 | async-start | bytes 2097152 | tf_op jit(solution)/shard_map/all_to_all | solution.py:144
  110.3 0.7 compare_and_fusion
  110.9 0.7 compare_and_fusion.1
  111.6 1.6 fusion.42
  113.3 2.1 %collective-permute-start.2 = (f32[64,512]{1,0:T(8,128)S(1)}, f32[64,512]{1,0:T(8,128)S(1)}, u32[]{:S(2)}, u32[]{:S(2)}) collective-permute-start(f32[64,512]{1,0:T(8,128)S(1)} %fusion.17), channel_id=1, source_target_pairs={{0,4},{4,8},{8,12},{12,16},{16,20},{20,24},{24,28},{28,0},{1,5},{5... | collective-permute-start | bytes 393224 | tf_op jit(solution)/shard_map/ppermute | solution.py:17
  115.6 22.0 %collective-permute-done.2 = f32[64,512]{1,0:T(8,128)S(1)} collective-permute-done((f32[64,512]{1,0:T(8,128)S(1)}, f32[64,512]{1,0:T(8,128)S(1)}, u32[]{:S(2)}, u32[]{:S(2)}) %collective-permute-start.2) | collective-permute-done | bytes 131104 | tf_op jit(solution)/shard_map/ppermute | solution.py:17
  138.3 0.7 copy.146
  139.1 0.7 copy.145
  140.1 5.1 %collective-permute-done.3 = f32[64,512]{1,0:T(8,128)S(1)} collective-permute-done((f32[64,512]{1,0:T(8,128)S(1)}, f32[64,512]{1,0:T(8,128)S(1)}, u32[]{:S(2)}, u32[]{:S(2)}) %collective-permute-start.3) | collective-permute-done | bytes 131104 | tf_op jit(solution)/shard_map/ppermute | solution.py:20
  145.4 1.3 scatter-add.9
  146.7 0.8 copy-done.3
  147.4 1.1 copy.100
  148.6 0.4 reshape.313
  149.1 14.1 %all-gather.3.cloned.1.call-done = f32[16,64,512]{2,1,0:T(8,128)} async-done(((f32[2,64,512]{2,1,0:T(8,128)}), f32[16,64,512]{2,1,0:T(8,128)}) %all-gather.3.cloned.1.call-update) | async-done | bytes 2097168 | tf_op jit(solution)/shard_map/all_gather | solution.py:137
  163.1 1.8 %reduce_sum.62 = f32[2,64,512]{2,1,0:T(8,128)S(1)} reduce(f32[8,2,64,512]{3,2,1,0:T(8,128)} %bitcast.109, f32[]{:T(128)} %constant.128.clone.1), dimensions={0}, to_apply=%region_8.9 | reduce | flops 458752 | bytes 2359300 | tf_op jit(solution)/shard_map/reduce_sum | solution.py:137
  165.5 0.7 fusion.44
  (68 shorter events, 4.4 us)
Async XLA Ops:
  11.4 13.3 %copy-start.7 = (s32[2]{0:T(128)S(1)}, s32[2]{0:T(128)}, u32[]{:S(2)}) copy-start(s32[2]{0:T(128)} %param.15) | copy-start | bytes 28
  11.4 15.2 %copy-start.5 = (bf16[256,256]{1,0:T(8,128)(2,1)S(1)}, bf16[256,256]{1,0:T(8,128)(2,1)}, u32[]{:S(2)}) copy-start(bf16[256,256]{1,0:T(8,128)(2,1)} %param.13) | copy-start | bytes 393220
  12.5 15.5 %copy-start.6 = (bf16[256,256]{1,0:T(8,128)(2,1)S(1)}, bf16[256,256]{1,0:T(8,128)(2,1)}, u32[]{:S(2)}) copy-start(bf16[256,256]{1,0:T(8,128)(2,1)} %param.10) | copy-start | bytes 393220
  12.5 64.0 %all-to-all-start = ((bf16[8,2,64,512]{3,2,1,0:T(8,128)(2,1)}), bf16[8,2,64,512]{3,2,1,0:T(8,128)(2,1)S(1)}, u32[]{:S(2)}, u32[]{:S(2)}) async-start(bf16[8,2,64,512]{3,2,1,0:T(8,128)(2,1)} %broadcast_select_fusion), calls=%async_computation | async-start | bytes 2097152 | tf_op jit(solution)/shard_map/all_to_all | solution.py:67
  19.9 143.2 %all-gather.3.cloned.1.call-start = ((), (), s32[]{:S(2)}) async-start(), calls=%async_computation.2 | async-start | bytes 2359296 | tf_op jit(solution)/shard_map/all_gather | solution.py:137
  20.0 53.4 %collective-permute-start.1 = (bf16[64,512]{1,0:T(8,128)(2,1)S(1)}, bf16[64,512]{1,0:T(8,128)(2,1)S(1)}, u32[]{:S(2)}, u32[]{:S(2)}) collective-permute-start(bf16[64,512]{1,0:T(8,128)(2,1)S(1)} %get-tuple-element.45), channel_id=1, source_target_pairs={{4,0},{8,4},{12,8},{16,12},{20,16},{24,20},{28,24},{0,28},{5,1},{9... | collective-permute-start | bytes 196616 | tf_op jit(solution)/shard_map/ppermute | solution.py:20
  24.7 48.7 %collective-permute-start = (bf16[64,512]{1,0:T(8,128)(2,1)S(1)}, bf16[64,512]{1,0:T(8,128)(2,1)S(1)}, u32[]{:S(2)}, u32[]{:S(2)}) collective-permute-start(bf16[64,512]{1,0:T(8,128)(2,1)S(1)} %get-tuple-element.46), channel_id=1, source_target_pairs={{0,4},{4,8},{8,12},{12,16},{16,20},{20,24},{24,28},{28,0},{1,5},{5... | collective-permute-start | bytes 196616 | tf_op jit(solution)/shard_map/ppermute | solution.py:17
  81.5 1.2 copy-start.1
  98.5 1.8 %copy-start = (f32[4,7,64,512]{3,2,1,0:T(8,128)}, f32[4,7,64,512]{3,2,1,0:T(8,128)S(1)}, u32[]{:S(2)}) copy-start(f32[4,7,64,512]{3,2,1,0:T(8,128)S(1)} %pad_maximum_fusion) | copy-start | bytes 11010052
  105.5 42.0 %all-to-all-start.1 = ((bf16[8,2,64,512]{3,1,2,0:T(2,128)(2,1)}), bf16[8,2,64,512]{3,1,2,0:T(2,128)(2,1)S(1)}, u32[]{:S(2)}, u32[]{:S(2)}) async-start(bf16[8,2,64,512]{3,1,2,0:T(2,128)(2,1)} %copy.99), calls=%async_computation.1 | async-start | bytes 2097152 | tf_op jit(solution)/shard_map/all_to_all | solution.py:144
  113.3 24.3 %collective-permute-start.2 = (f32[64,512]{1,0:T(8,128)S(1)}, f32[64,512]{1,0:T(8,128)S(1)}, u32[]{:S(2)}, u32[]{:S(2)}) collective-permute-start(f32[64,512]{1,0:T(8,128)S(1)} %fusion.17), channel_id=1, source_target_pairs={{0,4},{4,8},{8,12},{12,16},{16,20},{20,24},{24,28},{28,0},{1,5},{5... | collective-permute-start | bytes 393224 | tf_op jit(solution)/shard_map/ppermute | solution.py:17
  115.6 22.5 %copy-start.2 = (bf16[4,64,2,128]{3,1,2,0:T(8,128)(2,1)S(1)}, bf16[4,64,2,128]{3,1,2,0:T(8,128)(2,1)}, u32[]{:S(2)}) copy-start(bf16[4,64,2,128]{3,1,2,0:T(8,128)(2,1)} %get-tuple-element.56) | copy-start | bytes 393220
  137.7 7.5 %collective-permute-start.3 = (f32[64,512]{1,0:T(8,128)S(1)}, f32[64,512]{1,0:T(8,128)S(1)}, u32[]{:S(2)}, u32[]{:S(2)}) collective-permute-start(f32[64,512]{1,0:T(8,128)S(1)} %get-tuple-element.35), channel_id=1, source_target_pairs={{4,0},{8,4},{12,8},{16,12},{20,16},{24,20},{28,24},{0,28},{5,1},{9... | collective-permute-start | bytes 393224 | tf_op jit(solution)/shard_map/ppermute | solution.py:20
  146.7 0.8 copy-start.3
  149.0 15.9 %copy-start.4 = (f32[4,64,512]{2,0,1:T(4,128)S(1)}, f32[4,64,512]{2,0,1:T(4,128)}, u32[]{:S(2)}) copy-start(f32[4,64,512]{2,0,1:T(4,128)} %copy-done.3) | copy-start | bytes 1572868
Sparse Core Ops, SparseCore 0:
  101.3 61.8 all-gather.2
